TPU v7x, 256 devices: a whole 4x4x8 slice. The times are simulated.
256 devices in a mesh: hi: 8 (over x, core), lo: 32 (over y, z).
Axes of the slice: x: 4, y: 4, z: 8, core: 2. Of those that a mesh axis runs over, the one named last changes fastest.
Arguments:
- right_side: bfloat16 [32, 491520], P(None, ('hi', 'lo')), may hold values from -4.5 to 6.3125
- point_order: int32 [256, 1920], P(('hi', 'lo')), may hold values from 0 to 1919, each once within a row
- leaf_blocks: bfloat16 [491520, 1920], P(('hi', 'lo')), may hold values from -1 to 6
- bases: bfloat16 [8, 491520, 128], P(None, ('hi', 'lo')), may hold values from -1 to 1
Outputs:
- solution: float32 [32, 491520], P(None, ('hi', 'lo'))
All inputs are finite; a program needn't handle non-finite values.
Results may differ from a plain program's by a relative error of at most 0.0003.
Values sent between devices are 32-bit elements; how exact they have to be, the bound alone decides.
A program may use at most 64 MiB of HBM per device.

v0:
```python
import jax
import jax.numpy as jnp
from jax import lax
from jax.sharding import PartitionSpec as P

ITERS = 3


def partner(block, axis, apart):
    count = lax.axis_size(axis)
    route = []
    for low in range(count):
        high = low | 1 << apart
        if high != low and high < count:
            route += [(low, high), (high, low)]
    return lax.ppermute(block, axis, route)


def split_rows(vector, axis_pos):
    high_part = lax.optimization_barrier(vector.astype(jnp.bfloat16))
    low_part = (vector - high_part.astype(jnp.float32)).astype(jnp.bfloat16)
    return jnp.concatenate([high_part, low_part], axis=axis_pos)


def subtree_sums(projected):
    lower_bits = lax.axis_size("lo").bit_length() - 1
    siblings = []
    pending = projected
    for depth_bit in range(lower_bits):
        received = partner(pending, "lo", depth_bit)
        siblings.append(received[0])
        pending = pending[1:] + received[1:]
    upper_bits = lax.axis_size("hi").bit_length() - 1
    for depth_bit in range(upper_bits):
        received = partner(pending, "hi", depth_bit)
        siblings.append(received[0])
        pending = pending[1:] + received[1:]
    return jnp.stack(siblings)


def apply_operator(vector, leaf_blocks, bases):
    rhs_count = vector.shape[0]
    halves = split_rows(vector, 0)
    near_term = jnp.dot(halves, leaf_blocks, preferred_element_type=jnp.float32)
    projected = jnp.einsum("rp,lpc->lrc", halves, bases, preferred_element_type=jnp.float32)
    projected = projected[:, :rhs_count] + projected[:, rhs_count:]
    siblings = subtree_sums(projected)
    sibling_halves = split_rows(siblings, 1)
    far_term = jnp.einsum("lrc,lpc->rp", sibling_halves, bases, preferred_element_type=jnp.float32)
    combined = near_term + far_term
    return combined[:rhs_count] + combined[rhs_count:]


def squares(residual):
    return lax.psum(jnp.sum(residual * residual, axis=1), ("hi", "lo"))


def per_device(right_side, point_order, leaf_blocks, bases):
    tree_order = point_order[0]
    tree_rhs = jnp.take(right_side, tree_order, axis=1).astype(jnp.float32)
    solution = jnp.zeros_like(tree_rhs)
    residual = tree_rhs
    direction = tree_rhs
    norm_now = squares(residual)
    for iteration in range(ITERS):
        images = apply_operator(direction, leaf_blocks, bases)
        curvature = lax.psum(jnp.sum(direction * images, axis=1), ("hi", "lo"))
        step_size = norm_now / curvature
        solution = solution + step_size[:, None] * direction
        residual = residual - step_size[:, None] * images
        norm_next = squares(residual)
        direction = residual + (norm_next / norm_now)[:, None] * direction
        norm_now = norm_next
    return jnp.zeros_like(solution).at[:, tree_order].set(solution)


def solution(mesh):
    in_specs = (
        P(None, ("hi", "lo")),
        P(("hi", "lo"), None),
        P(("hi", "lo"), None),
        P(None, ("hi", "lo"), None),
    )
    out_specs = P(None, ("hi", "lo"))
    return jax.shard_map(
        per_device, mesh=mesh, in_specs=in_specs, out_specs=out_specs, check_vma=False
    )
```

profile of v0, /device:TPU:1, one launch (start us, length us, event | category | flops | bytes accessed | tf_op | source)
XLA Modules:
  0.0 555.1 jit_solution(14598960404362432203)
XLA Ops:
  2.1 2.0 copy.9
  4.1 5.6 %gather_fusion = bf16[1920,32]{1,0:T(8,128)(2,1)} fusion(bf16[32,1920]{0,1:T(8,128)(2,1)} %copy.9, s32[2048]{0:T(1024)S(1)} %pad_clamp_fusion), kind=kCustom, calls=%fused_computation | custom fusion | bytes 253440 | tf_op jit(solution)/shard_map/jit(_take)/gather | solution.py:60
  9.7 1.2 copy.10
  11.1 3.1 convolution_bitcast_fusion.5
  14.2 2.6 collective-permute-start
  16.7 2.4 collective-permute-done
  19.1 3.8 collective-permute-start.1
  22.9 3.4 collective-permute-done.1
  26.4 7.9 %collective-permute-start.2 = (f32[6,32,128]{2,1,0:T(8,128)S(1)}, f32[6,32,128]{2,1,0:T(8,128)S(1)}, u32[]{:S(2)}, u32[]{:S(2)}) collective-permute-start(f32[6,32,128]{2,1,0:T(8,128)S(1)} %slice_add_fusion.11), channel_id=1, source_target_pairs={{0,4},{4,0},{1,5},{5,1},{2,6},{6,2},{3,7},{7,3},{8,12},{12,8},{9,1... | collective-permute-start | bytes 294920 | tf_op jit(solution)/shard_map/ppermute | solution.py:16
  34.3 2.1 collective-permute-done.2
  36.4 1.4 collective-permute-start.3
  37.8 2.0 collective-permute-done.3
  39.8 3.0 collective-permute-start.4
  42.8 1.7 collective-permute-done.4
  44.5 5.2 collective-permute-start.5
  49.7 0.9 collective-permute-done.5
  50.6 1.2 collective-permute-start.6
  51.8 1.5 collective-permute-done.6
  53.3 2.8 collective-permute-start.7
  56.1 1.3 collective-permute-done.7
  57.5 1.3 convolution_bitcast_fusion.2
  58.8 1.3 convolution_add_fusion.2
  60.3 79.5 %all-reduce = (f32[32]{0:T(128)S(1)}, f32[32]{0:T(128)S(1)}) all-reduce(f32[32]{0:T(128)S(1)} %get-tuple-element.6, f32[32]{0:T(128)S(1)} %get-tuple-element.5), channel_id=1, replica_groups=mesh['hi'=8,'lo'=32] {'hi','lo'}, use_global_device_ids=true, to_apply=%region_1.2 | all-reduce | flops 64 | bytes 512 | tf_op jit(solution)/shard_map/psum | solution.py:55
  140.0 73.4 %psum.44 = f32[32]{0:T(128)S(1)} all-reduce(f32[32]{0:T(128)S(1)} %multiply_reduce_fusion.2), channel_id=1, replica_groups=mesh['hi'=8,'lo'=32] {'hi','lo'}, use_global_device_ids=true, to_apply=%region_5.6 | all-reduce | flops 32 | bytes 256 | tf_op jit(solution)/shard_map/psum | solution.py:55
  213.7 3.1 convolution_bitcast_fusion.4
  216.8 1.9 collective-permute-start.8
  218.7 3.2 collective-permute-done.8
  222.1 6.2 %collective-permute-done.9 = f32[7,32,128]{2,1,0:T(8,128)S(1)} collective-permute-done((f32[7,32,128]{2,1,0:T(8,128)S(1)}, f32[7,32,128]{2,1,0:T(8,128)S(1)}, u32[]{:S(2)}, u32[]{:S(2)}) %collective-permute-start.9) | collective-permute-done | bytes 114720 | tf_op jit(solution)/shard_map/ppermute | solution.py:16
  228.3 3.9 collective-permute-start.10
  232.2 4.2 collective-permute-done.10
  236.4 0.9 collective-permute-start.11
  237.3 2.6 collective-permute-done.11
  239.9 1.8 collective-permute-start.12
  241.7 3.0 collective-permute-done.12
  244.7 6.4 %collective-permute-start.13 = (f32[3,32,128]{2,1,0:T(8,128)S(1)}, f32[3,32,128]{2,1,0:T(8,128)S(1)}, u32[]{:S(2)}, u32[]{:S(2)}) collective-permute-start(f32[3,32,128]{2,1,0:T(8,128)S(1)} %slice_add_fusion.19), channel_id=1, source_target_pairs={{0,32},{32,0},{64,96},{96,64},{128,160},{160,128},{192,224},{224,1... | collective-permute-start | bytes 147464 | tf_op jit(solution)/shard_map/ppermute | solution.py:16
  251.1 0.9 collective-permute-done.13
  252.2 2.5 collective-permute-done.14
  254.7 1.3 collective-permute-start.15
  256.0 2.8 collective-permute-done.15
  258.9 1.3 convolution_bitcast_fusion.1
  260.2 4.4 convolution_add_fusion.1
  266.1 75.9 %psum.45 = f32[32]{0:T(128)} all-reduce(f32[32]{0:T(128)} %multiply_reduce_fusion.1), channel_id=1, replica_groups=mesh['hi'=8,'lo'=32] {'hi','lo'}, use_global_device_ids=true, to_apply=%region_7.8 | all-reduce | flops 32 | bytes 256 | tf_op jit(solution)/shard_map/psum | solution.py:67
  343.1 2.5 multiply_reduce_fusion
  345.7 72.4 %psum.46 = f32[32]{0:T(128)} all-reduce(f32[32]{0:T(128)} %get-tuple-element.11), channel_id=1, replica_groups=mesh['hi'=8,'lo'=32] {'hi','lo'}, use_global_device_ids=true, to_apply=%region_9.10 | all-reduce | flops 32 | bytes 256 | tf_op jit(solution)/shard_map/psum | solution.py:55
  418.8 1.1 fusion.34
  419.9 3.1 convolution_bitcast_fusion.3
  423.0 1.9 collective-permute-start.16
  424.9 3.2 collective-permute-done.16
  428.9 5.7 %collective-permute-done.17 = f32[7,32,128]{2,1,0:T(8,128)S(1)} collective-permute-done((f32[7,32,128]{2,1,0:T(8,128)S(1)}, f32[7,32,128]{2,1,0:T(8,128)S(1)}, u32[]{:S(2)}, u32[]{:S(2)}) %collective-permute-start.17) | collective-permute-done | bytes 114720 | tf_op jit(solution)/shard_map/ppermute | solution.py:16
  434.5 2.8 collective-permute-start.18
  437.3 5.2 collective-permute-done.18
  443.3 2.9 collective-permute-done.19
  446.2 1.3 collective-permute-start.20
  447.5 3.4 collective-permute-done.20
  450.9 6.8 %collective-permute-start.21 = (f32[3,32,128]{2,1,0:T(8,128)S(1)}, f32[3,32,128]{2,1,0:T(8,128)S(1)}, u32[]{:S(2)}, u32[]{:S(2)}) collective-permute-start(f32[3,32,128]{2,1,0:T(8,128)S(1)} %slice_add_fusion.18), channel_id=1, source_target_pairs={{0,32},{32,0},{64,96},{96,64},{128,160},{160,128},{192,224},{224,1... | collective-permute-start | bytes 147464 | tf_op jit(solution)/shard_map/ppermute | solution.py:16
  457.8 0.9 collective-permute-done.21
  458.7 2.7 collective-permute-done.22
  462.2 3.3 collective-permute-done.23
  465.6 1.3 convolution_bitcast_fusion
  466.9 1.3 convolution_add_fusion
  468.3 75.2 %psum.47 = f32[32]{0:T(128)S(1)} all-reduce(f32[32]{0:T(128)S(1)} %fusion.10), channel_id=1, replica_groups=mesh['hi'=8,'lo'=32] {'hi','lo'}, use_global_device_ids=true, to_apply=%region_11.12 | all-reduce | flops 32 | bytes 256 | tf_op jit(solution)/shard_map/psum | solution.py:67
  544.2 1.1 fusion.7
  545.7 8.4 %scatter_custom_fusion = f32[32,1920]{0,1:T(8,128)S(1)} fusion(s32[1920]{0:T(1024)} %copy-done.5, f32[1920,32]{1,0:T(8,128)S(1)} %copy.11, f32[]{:T(128)} %constant.6.clone.1), kind=kCustom, calls=%fused_computation.17 | custom fusion | bytes 246272 | tf_op jit(solution)/shard_map/scatter | solution.py:74
  554.1 1.0 copy.12
  (104 shorter events, 10.4 us)
Async XLA Ops:
  0.7 0.6 copy-start.5
  2.1 56.7 %slice-start = ((s8[7372800]{0:T(1024)(128)(4,1)}), s8[3178496]{0:T(1024)(128)(4,1)S(1)}, s32[]{:S(2)}) async-start(s8[7372800]{0:T(1024)(128)(4,1)} %bitcast.55), calls=%async_computation | async-start | bytes 6356992
  11.0 46.5 %copy-start = (bf16[8,1920,128]{2,1,0:T(8,128)(2,1)S(1)}, bf16[8,1920,128]{2,1,0:T(8,128)(2,1)}, u32[]{:S(2)}) copy-start(bf16[8,1920,128]{2,1,0:T(8,128)(2,1)} %param.7) | copy-start | bytes 11796484
  11.1 47.7 %slice-start.1 = ((s8[7372800]{0:T(1024)(128)(4,1)}), s8[4194304]{0:T(1024)(128)(4,1)S(1)}, s32[]{:S(2)}) async-start(s8[7372800]{0:T(1024)(128)(4,1)} %bitcast.55), calls=%async_computation.1 | async-start | bytes 8388608
  14.2 4.9 collective-permute-start
  19.1 7.2 %collective-permute-start.1 = (f32[7,32,128]{2,1,0:T(8,128)S(1)}, f32[7,32,128]{2,1,0:T(8,128)S(1)}, u32[]{:S(2)}, u32[]{:S(2)}) collective-permute-start(f32[7,32,128]{2,1,0:T(8,128)S(1)} %slice_add_fusion.8), channel_id=1, source_target_pairs={{0,2},{2,0},{1,3},{3,1},{4,6},{6,4},{5,7},{7,5},{8,10},{10,8},{9,1... | collective-permute-start | bytes 344072 | tf_op jit(solution)/shard_map/ppermute | solution.py:16
  26.4 10.0 %collective-permute-start.2 = (f32[6,32,128]{2,1,0:T(8,128)S(1)}, f32[6,32,128]{2,1,0:T(8,128)S(1)}, u32[]{:S(2)}, u32[]{:S(2)}) collective-permute-start(f32[6,32,128]{2,1,0:T(8,128)S(1)} %slice_add_fusion.11), channel_id=1, source_target_pairs={{0,4},{4,0},{1,5},{5,1},{2,6},{6,2},{3,7},{7,3},{8,12},{12,8},{9,1... | collective-permute-start | bytes 294920 | tf_op jit(solution)/shard_map/ppermute | solution.py:16
  36.4 3.4 collective-permute-start.3
  39.8 4.7 collective-permute-start.4
  44.5 6.1 %collective-permute-start.5 = (f32[3,32,128]{2,1,0:T(8,128)S(1)}, f32[3,32,128]{2,1,0:T(8,128)S(1)}, u32[]{:S(2)}, u32[]{:S(2)}) collective-permute-start(f32[3,32,128]{2,1,0:T(8,128)S(1)} %slice_add_fusion.20), channel_id=1, source_target_pairs={{0,32},{32,0},{64,96},{96,64},{128,160},{160,128},{192,224},{224,1... | collective-permute-start | bytes 147464 | tf_op jit(solution)/shard_map/ppermute | solution.py:16
  50.6 2.8 collective-permute-start.6
  53.3 4.1 collective-permute-start.7
  213.4 45.4 %copy-start.8 = (f32[32]{0:T(128)}, f32[32]{0:T(128)S(1)}, u32[]{:S(2)}) copy-start(f32[32]{0:T(128)S(1)} %psum.44) | copy-start | bytes 388
  213.4 51.1 %copy-start.6 = (f32[32]{0:T(128)}, f32[32]{0:T(128)S(1)}, u32[]{:S(2)}) copy-start(f32[32]{0:T(128)S(1)} %div.16) | copy-start | bytes 388
  213.4 45.4 %copy-start.1 = (bf16[8,1920,128]{2,1,0:T(8,128)(2,1)S(1)}, bf16[8,1920,128]{2,1,0:T(8,128)(2,1)}, u32[]{:S(2)}) copy-start(bf16[8,1920,128]{2,1,0:T(8,128)(2,1)} %param.7) | copy-start | bytes 11796484
  216.8 5.1 collective-permute-start.8
  221.9 6.4 %collective-permute-start.9 = (f32[7,32,128]{2,1,0:T(8,128)S(1)}, f32[7,32,128]{2,1,0:T(8,128)S(1)}, u32[]{:S(2)}, u32[]{:S(2)}) collective-permute-start(f32[7,32,128]{2,1,0:T(8,128)S(1)} %slice_add_fusion.7), channel_id=1, source_target_pairs={{0,2},{2,0},{1,3},{3,1},{4,6},{6,4},{5,7},{7,5},{8,10},{10,8},{9,1... | collective-permute-start | bytes 344072 | tf_op jit(solution)/shard_map/ppermute | solution.py:16
  228.3 8.1 %collective-permute-start.10 = (f32[6,32,128]{2,1,0:T(8,128)S(1)}, f32[6,32,128]{2,1,0:T(8,128)S(1)}, u32[]{:S(2)}, u32[]{:S(2)}) collective-permute-start(f32[6,32,128]{2,1,0:T(8,128)S(1)} %slice_add_fusion.10), channel_id=1, source_target_pairs={{0,4},{4,0},{1,5},{5,1},{2,6},{6,2},{3,7},{7,3},{8,12},{12,8},{9,1... | collective-permute-start | bytes 294920 | tf_op jit(solution)/shard_map/ppermute | solution.py:16
  236.4 3.6 collective-permute-start.11
  239.9 4.7 collective-permute-start.12
  244.7 7.3 %collective-permute-start.13 = (f32[3,32,128]{2,1,0:T(8,128)S(1)}, f32[3,32,128]{2,1,0:T(8,128)S(1)}, u32[]{:S(2)}, u32[]{:S(2)}) collective-permute-start(f32[3,32,128]{2,1,0:T(8,128)S(1)} %slice_add_fusion.19), channel_id=1, source_target_pairs={{0,32},{32,0},{64,96},{96,64},{128,160},{160,128},{192,224},{224,1... | collective-permute-start | bytes 147464 | tf_op jit(solution)/shard_map/ppermute | solution.py:16
  251.9 2.8 collective-permute-start.14
  254.7 4.1 collective-permute-start.15
  264.6 0.8 copy-start.3
  265.3 201.5 %slice-start.2 = ((s8[7372800]{0:T(1024)(128)(4,1)}), s8[3178496]{0:T(1024)(128)(4,1)S(1)}, s32[]{:S(2)}) async-start(s8[7372800]{0:T(1024)(128)(4,1)} %bitcast.57), calls=%async_computation.2 | async-start | bytes 6356992
  342.6 0.5 copy-start.7
  419.8 48.3 %copy-start.4 = (f32[32,1920]{1,0:T(8,128)}, f32[32,1920]{1,0:T(8,128)S(1)}, u32[]{:S(2)}) copy-start(f32[32,1920]{1,0:T(8,128)S(1)} %get-tuple-element.10) | copy-start | bytes 737284
  419.9 45.7 %copy-start.2 = (bf16[8,1920,128]{2,1,0:T(8,128)(2,1)S(1)}, bf16[8,1920,128]{2,1,0:T(8,128)(2,1)}, u32[]{:S(2)}) copy-start(bf16[8,1920,128]{2,1,0:T(8,128)(2,1)} %param.7) | copy-start | bytes 11796484
  419.9 47.0 %slice-start.3 = ((s8[7372800]{0:T(1024)(128)(4,1)}), s8[4194304]{0:T(1024)(128)(4,1)S(1)}, s32[]{:S(2)}) async-start(s8[7372800]{0:T(1024)(128)(4,1)} %bitcast.57), calls=%async_computation.3 | async-start | bytes 8388608
  423.0 5.1 collective-permute-start.16
  428.2 6.4 %collective-permute-start.17 = (f32[7,32,128]{2,1,0:T(8,128)S(1)}, f32[7,32,128]{2,1,0:T(8,128)S(1)}, u32[]{:S(2)}, u32[]{:S(2)}) collective-permute-start(f32[7,32,128]{2,1,0:T(8,128)S(1)} %slice_add_fusion.6), channel_id=1, source_target_pairs={{0,2},{2,0},{1,3},{3,1},{4,6},{6,4},{5,7},{7,5},{8,10},{10,8},{9,1... | collective-permute-start | bytes 344072 | tf_op jit(solution)/shard_map/ppermute | solution.py:16
  434.5 8.0 %collective-permute-start.18 = (f32[6,32,128]{2,1,0:T(8,128)S(1)}, f32[6,32,128]{2,1,0:T(8,128)S(1)}, u32[]{:S(2)}, u32[]{:S(2)}) collective-permute-start(f32[6,32,128]{2,1,0:T(8,128)S(1)} %slice_add_fusion.9), channel_id=1, source_target_pairs={{0,4},{4,0},{1,5},{5,1},{2,6},{6,2},{3,7},{7,3},{8,12},{12,8},{9,1... | collective-permute-start | bytes 294920 | tf_op jit(solution)/shard_map/ppermute | solution.py:16
  442.6 3.6 collective-permute-start.19
  446.2 4.7 collective-permute-start.20
  450.9 7.7 %collective-permute-start.21 = (f32[3,32,128]{2,1,0:T(8,128)S(1)}, f32[3,32,128]{2,1,0:T(8,128)S(1)}, u32[]{:S(2)}, u32[]{:S(2)}) collective-permute-start(f32[3,32,128]{2,1,0:T(8,128)S(1)} %slice_add_fusion.18), channel_id=1, source_target_pairs={{0,32},{32,0},{64,96},{96,64},{128,160},{160,128},{192,224},{224,1... | collective-permute-start | bytes 147464 | tf_op jit(solution)/shard_map/ppermute | solution.py:16
  458.6 2.8 collective-permute-start.22
  461.4 4.1 collective-permute-start.23
where the time goes:
time: 556 us; the launch traced here: 555 us
  blocking collectives  377 us (68%)
  waiting for transfers between devices  68 us (12%)
  starting transfers between devices  59.3 us (11%)
  local copies, waits for them, and re-layouts  20.6 us (4%)
  matrix products  20 us (4%)
  other arithmetic  10.2 us (2%)
    psum x3, blocking collectives, squares(): return lax.psum(jnp.sum(residual * residual, axis=1), ('hi', 'lo'))  225 us
    psum x2, blocking collectives, per_device(): curvature = lax.psum(jnp.sum(direction * images, axis=1), ('hi', 'lo'))  151 us
    ppermute x24, waiting for transfers between devices, partner(): return lax.ppermute(block, axis, route)  68 us
    ppermute x24, starting transfers between devices, partner(): return lax.ppermute(block, axis, route)  59.3 us
  transfers between devices with their start and end apart: 24, of which 24 were waited for; matrix products, arithmetic and copies ran while one was open for 0% of the time, Pallas kernels for 0%

commit v1 on v0

v1 whole, which is shorter than its diff:
```python
import functools

import jax
import jax.numpy as jnp
from jax import lax
from jax.experimental import pallas as pl
from jax.experimental.pallas import tpu as pltpu
from jax.sharding import PartitionSpec as P

ITERS = 3
Z_COUNT = 8
MESH = pl.DeviceIdType.MESH
F32 = jnp.float32
BF16 = jnp.bfloat16
NN = (((1,), (0,)), ((), ()))
NT = (((1,), (1,)), ((), ()))


def bits(count):
    return count.bit_length() - 1


def spans(total, width):
    return [(low, min(width, total - low)) for low in range(0, total, width)]


def split(value):
    high = value.astype(BF16)
    low = (value - high.astype(F32)).astype(BF16)
    return high, low


def product(left, right, numbers):
    rows = left.shape[0] // 2
    both = lax.dot_general(left, right, numbers, preferred_element_type=F32)
    return both[:rows] + both[rows:]


def row_dot(a, b):
    return jnp.sum(a * b, axis=1, keepdims=True)


def pack_columns(columns):
    groups = columns[0].shape[0] // 8
    lane = lax.broadcasted_iota(jnp.int32, (8, 128), 1)
    tile = jnp.zeros((8, 128), F32)
    for kind, column in enumerate(columns):
        for group in range(groups):
            part = column[8 * group:8 * group + 8]
            tile = jnp.where(lane == kind * groups + group, part, tile)
    return tile


def unpack_column(tile, kind, groups):
    first = kind * groups
    parts = [tile[:, first + group:first + group + 1] for group in range(groups)]
    return jnp.concatenate(parts, axis=0)


def tree_steps(blocks, first_level, per_level):
    rows = blocks[0].shape[0]
    level_of_row = lax.broadcasted_iota(jnp.int32, (rows, 128), 0) // per_level
    products = jnp.zeros((rows, 128), F32)
    node_sums = []
    current = blocks
    level = first_level
    while len(current) > 1:
        node_sums.append(current)
        pairs = [(current[m], current[m + 1]) for m in range(0, len(current), 2)]
        total = sum(a * b for a, b in pairs)
        products = products + jnp.where(level_of_row == level, total, 0.0)
        current = [a + b for a, b in pairs]
        level += 1
    return node_sums, current[0], products


def fold_levels(products, per_level):
    column = jnp.sum(products, axis=1, keepdims=True)
    total = column[:per_level]
    for low in range(per_level, products.shape[0], per_level):
        total = total + column[low:low + per_level]
    return 2.0 * total


def kernel(dims, rhs_ref, order_ref, leaf_hbm, bases_hbm, out_ref, *scratch):
    nz, ny, nh = dims
    (blocks, basis, onehot, halves, sib_f32, sib_halves, residual, direction, image, far_dir,
     near, placed, pending, near_send, z_recv, y_send, y_recv, h_send, h_recv, a_send, a_recv, b_send,
     b_recv, last_recv, load_sem, send_sem, recv_sem) = scratch
    rhs_count, leaf = residual.shape
    levels = bases_hbm.shape[0]
    own = rhs_count // nz
    groups = rhs_count // 8
    zb, yb = bits(nz), bits(ny)
    z_rows = levels * own
    h_low = (zb + yb) * own // 8 * 8
    a_rows = zb * own

    hi = lax.axis_index("hi")
    lo = lax.axis_index("lo")
    z = lax.rem(lo, nz)
    y = lo // nz

    def z_peer(step):
        return lax.rem(z + step, nz)

    def y_peer(step):
        return lax.rem(y + step, ny)

    def h_peer(step):
        return lax.rem(hi + step, nh)

    partners = [(hi, y * nz + z_peer(step)) for step in range(1, nz)]
    partners += [(hi, y_peer(step) * nz + z) for step in range(1, ny)]
    partners += [(h_peer(step), lo) for step in range(1, nh)]

    loads = []
    for level in range(levels):
        loads.append(pltpu.make_async_copy(
            bases_hbm.at[level], basis.at[:, pl.ds(128 * level, 128)], load_sem.at[level]))
    loads.append(pltpu.make_async_copy(leaf_hbm, blocks, load_sem.at[levels]))
    for load in loads:
        load.start()

    barrier = pltpu.get_barrier_semaphore()
    for partner in partners:
        pl.semaphore_signal(barrier, inc=1, device_id=partner, device_id_type=MESH)

    def send(src, dst, t, phase, partner):
        pltpu.make_async_remote_copy(
            src_ref=src, dst_ref=dst, send_sem=send_sem.at[t, phase],
            recv_sem=recv_sem.at[t, phase], device_id=partner, device_id_type=MESH,
        ).start()

    def await_recv(slots, t, phase):
        pltpu.make_async_copy(slots, slots, recv_sem.at[t, phase]).wait()

    def await_send(slots, t, phase):
        pltpu.make_async_copy(slots, slots, send_sem.at[t, phase]).wait()

    order_row = order_ref[...]
    for low, width in spans(leaf, 128):
        place = lax.broadcasted_iota(jnp.int32, (width, leaf), 0) + low
        onehot[pl.ds(low, width), :] = jnp.where(place == order_row, 1.0, 0.0).astype(BF16)
    rhs_now = rhs_ref[...]
    for low, width in spans(leaf, 384):
        columns = pl.ds(low, width)
        tree = lax.dot_general(rhs_now, onehot[:, columns], NN, preferred_element_type=F32)
        residual[:, columns] = tree
        high, small = split(tree)
        halves[:, columns] = jnp.concatenate([high, small], axis=0)
    direction[...] = jnp.zeros_like(direction)
    image[...] = jnp.zeros_like(image)
    far_dir[...] = jnp.zeros_like(far_dir)
    placed[...] = jnp.zeros_like(placed)
    out_ref[...] = jnp.zeros_like(out_ref)

    for load in loads[:levels]:
        load.wait()

    def exchange(t, first, last):
        projected = product(halves[...], basis[...], NN)
        for j in range(nz):
            for level in range(levels):
                near_send[t, j, own * level:own * level + own, :] = (
                    projected[own * j:own * j + own, 128 * level:128 * level + 128])
        if first:
            pl.semaphore_wait(barrier, len(partners))
        for step in range(1, nz):
            peer = z_peer(step)
            send(near_send.at[t, peer], z_recv.at[t, z], t, 0, (hi, y * nz + peer))
        z_recv[t, z] = near_send[t, z]
        if first:
            loads[levels].wait()

        rr = jnp.zeros((rhs_count, 1), F32)
        rn = jnp.zeros((rhs_count, 1), F32)
        cross = jnp.zeros((rhs_count, 1), F32)
        for low, width in spans(leaf, 384):
            columns = pl.ds(low, width)
            near_now = product(halves[...], blocks[:, columns], NN)
            near[:, columns] = near_now
            r_now = residual[:, columns]
            rr = rr + row_dot(r_now, r_now)
            rn = rn + row_dot(r_now, near_now)
            cross = cross + row_dot(r_now, image[:, columns] + far_dir[:, columns])
            cross = cross + row_dot(direction[:, columns], near_now)
        tile = pack_columns([rr, rn, cross])

        lane = lax.broadcasted_iota(jnp.int32, (8, 128), 1)
        sub = lax.broadcasted_iota(jnp.int32, (8, 128), 0)
        mine = (lane == groups + z * own // 8) & (sub // own == lax.rem(z, 8 // own))

        def add_products(tile, products):
            dots = fold_levels(products, own)
            repeated = jnp.concatenate([dots] * (8 // own), axis=0)
            return tile + jnp.where(mine, repeated, 0.0)

        await_recv(z_recv.at[t, pl.ds(0, nz - 1)], t, 0)
        node_sums, total, products = tree_steps([z_recv[t, j] for j in range(nz)], 0, own)
        tile = add_products(tile, products)
        y_send[t, 0:8] = tile
        y_send[t, 8:z_rows] = total[8:]
        for step in range(1, ny):
            peer = y_peer(step)
            send(y_send.at[t], y_recv.at[t, y], t, 1, (hi, peer * nz + z))
        y_recv[t, y] = y_send[t]
        if not last:
            for j in range(nz):
                for level in range(zb):
                    rows = slice(own * level, own * level + own)
                    a_send[t, j, rows] = node_sums[level][(j >> level) ^ 1][rows]
            for step in range(1, nz):
                peer = z_peer(step)
                send(a_send.at[t, peer], a_recv.at[t, z], t, 3, (hi, y * nz + peer))
            a_recv[t, z] = a_send[t, z]

        if not first:
            place_chunk(0)

        await_recv(y_recv.at[t, pl.ds(0, ny - 1)], t, 1)
        _, total, products = tree_steps([y_recv[t, j] for j in range(ny)], zb, own)
        tile = add_products(total[0:8], products)
        h_send[t, 0:8] = tile
        h_send[t, 8:] = total[h_low:]
        for step in range(1, nh):
            send(h_send.at[t], h_recv.at[t, hi], t, 2, (h_peer(step), lo))
        h_recv[t, hi] = h_send[t]
        if not last:
            for level in range(yb):
                rows = slice(own * (zb + level), own * (zb + level) + own)
                first_node = ((y >> level) + 1 - 2 * lax.rem(y >> level, 2)) << level
                found = y_recv[t, first_node, rows]
                for extra in range(1, 1 << level):
                    found = found + y_recv[t, first_node + extra, rows]
                b_send[t, rows] = found

        if not first:
            place_chunk(1)

        await_recv(h_recv.at[t, pl.ds(0, nh - 1)], t, 2)
        first_hi = (zb + yb) * own - h_low + 8
        blocks_h = [h_recv[t, j] for j in range(nh)]
        _, total, products = tree_steps(blocks_h, first_hi // own, own)
        tile = add_products(total[0:8], products)
        b_send[t, 0:8] = tile
        if last:
            for step in range(1, nz):
                peer = z_peer(step)
                send(b_send.at[t, pl.ds(0, 8)], last_recv.at[z], t, 4, (hi, y * nz + peer))
            last_recv[z] = tile
            place_chunk(2)
            await_recv(last_recv.at[pl.ds(0, nz - 1)], t, 4)
            tile = sum(last_recv[j] for j in range(nz))
        else:
            for level in range(bits(nh)):
                rows = slice(own * (zb + yb + level), own * (zb + yb + level) + own)
                from_rows = slice(first_hi + own * level, first_hi + own * level + own)
                first_node = ((hi >> level) + 1 - 2 * lax.rem(hi >> level, 2)) << level
                found = h_recv[t, first_node, from_rows]
                for extra in range(1, 1 << level):
                    found = found + h_recv[t, first_node + extra, from_rows]
                b_send[t, rows] = found
            for step in range(1, nz):
                peer = z_peer(step)
                send(b_send.at[t], b_recv.at[t, z], t, 4, (hi, y * nz + peer))
            b_recv[t, z] = b_send[t]
            if not first:
                place_chunk(2)
            await_recv(a_recv.at[t, pl.ds(0, nz - 1)], t, 3)
            await_recv(b_recv.at[t, pl.ds(0, nz - 1)], t, 4)
            tile = b_recv[t, 0, 0:8]
            for j in range(1, nz):
                tile = tile + b_recv[t, j, 0:8]
            for j in range(nz):
                for level in range(levels):
                    source = a_recv if level < zb else b_recv
                    sib_f32[own * j:own * j + own, 128 * level:128 * level + 128] = (
                        source[t, j, own * level:own * level + own, :])
            high, small = split(sib_f32[...])
            sib_halves[...] = jnp.concatenate([high, small], axis=0)
        return [unpack_column(tile, kind, groups) for kind in range(3)]

    third = leaf // 3

    def place_chunk(number):
        for low, width in spans(third, 640):
            rows = pl.ds(number * third + low, width)
            pending[:, rows] = product(halves[...], onehot[rows, :], NT)

    rr_old = jnp.ones((rhs_count, 1), F32)
    curvature = jnp.zeros((rhs_count, 1), F32)
    for t in range(ITERS):
        first, last = t == 0, t == ITERS - 1
        rr, rn, cross = exchange(t, first, last)
        beta = jnp.zeros_like(rr) if first else rr / rr_old
        curvature = rn + beta * cross + beta * beta * curvature
        alpha = rr / curvature
        rr_old = rr
        here = rhs_now.astype(F32) if first else pending[...]
        place_now = here + beta * placed[...]
        placed[...] = place_now
        out_ref[...] = out_ref[...] + alpha * place_now
        if last:
            break
        for low, width in spans(leaf, 384):
            columns = pl.ds(low, width)
            far = product(sib_halves[...], basis[columns, :], NT)
            far_now = far + beta * far_dir[:, columns]
            far_dir[:, columns] = far_now
            image_now = near[:, columns] + far + beta * image[:, columns]
            image[:, columns] = image_now
            r_now = residual[:, columns]
            direction[:, columns] = r_now + beta * direction[:, columns]
            r_next = r_now - alpha * image_now
            residual[:, columns] = r_next
            high, small = split(r_next)
            halves[:, columns] = jnp.concatenate([high, small], axis=0)

    for t in range(ITERS):
        await_send(z_recv.at[t, pl.ds(0, nz - 1)], t, 0)
        await_send(y_recv.at[t, pl.ds(0, ny - 1)], t, 1)
        await_send(h_recv.at[t, pl.ds(0, nh - 1)], t, 2)
        if t < ITERS - 1:
            await_send(a_recv.at[t, pl.ds(0, nz - 1)], t, 3)
            await_send(b_recv.at[t, pl.ds(0, nz - 1)], t, 4)
        else:
            await_send(last_recv.at[pl.ds(0, nz - 1)], t, 4)


def per_device(dims, right_side, point_order, leaf_blocks, bases):
    nz, ny, nh = dims
    rhs_count, leaf = right_side.shape
    levels = bases.shape[0]
    own = rhs_count // nz
    z_rows = levels * own
    h_rows = 8 + z_rows - (bits(nz) + bits(ny)) * own // 8 * 8
    a_rows = bits(nz) * own
    vector = pltpu.VMEM((rhs_count, leaf), F32)
    scratch = [
        pltpu.VMEM((leaf, leaf), BF16),
        pltpu.VMEM((leaf, 128 * levels), BF16),
        pltpu.VMEM((leaf, leaf), BF16),
        pltpu.VMEM((2 * rhs_count, leaf), BF16),
        pltpu.VMEM((rhs_count, 128 * levels), F32),
        pltpu.VMEM((2 * rhs_count, 128 * levels), BF16),
        vector, vector, vector, vector, vector, vector, vector,
        pltpu.VMEM((ITERS, nz, z_rows, 128), F32),
        pltpu.VMEM((ITERS, nz, z_rows, 128), F32),
        pltpu.VMEM((ITERS, z_rows, 128), F32),
        pltpu.VMEM((ITERS, ny, z_rows, 128), F32),
        pltpu.VMEM((ITERS, h_rows, 128), F32),
        pltpu.VMEM((ITERS, nh, h_rows, 128), F32),
        pltpu.VMEM((ITERS, nz, a_rows, 128), F32),
        pltpu.VMEM((ITERS, nz, a_rows, 128), F32),
        pltpu.VMEM((ITERS, z_rows, 128), F32),
        pltpu.VMEM((ITERS, nz, z_rows, 128), F32),
        pltpu.VMEM((nz, 8, 128), F32),
        pltpu.SemaphoreType.DMA((levels + 1,)),
        pltpu.SemaphoreType.DMA((ITERS, 5)),
        pltpu.SemaphoreType.DMA((ITERS, 5)),
    ]
    return pl.pallas_call(
        functools.partial(kernel, dims),
        out_shape=jax.ShapeDtypeStruct((rhs_count, leaf), F32),
        in_specs=[
            pl.BlockSpec(memory_space=pltpu.VMEM),
            pl.BlockSpec(memory_space=pltpu.VMEM),
            pl.BlockSpec(memory_space=pl.ANY),
            pl.BlockSpec(memory_space=pl.ANY),
        ],
        out_specs=pl.BlockSpec(memory_space=pltpu.VMEM),
        scratch_shapes=scratch,
        compiler_params=pltpu.CompilerParams(
            collective_id=0, has_side_effects=True, vmem_limit_bytes=48 * 1024 * 1024
        ),
        name="tree_cg",
    )(right_side, point_order, leaf_blocks, bases)


def solution(mesh):
    dims = (Z_COUNT, mesh.shape["lo"] // Z_COUNT, mesh.shape["hi"])
    in_specs = (
        P(None, ("hi", "lo")),
        P(("hi", "lo"), None),
        P(("hi", "lo"), None),
        P(None, ("hi", "lo"), None),
    )
    return jax.shard_map(
        functools.partial(per_device, dims), mesh=mesh, in_specs=in_specs,
        out_specs=P(None, ("hi", "lo")), check_vma=False
    )
```

time: 556 us -> 79.6 us (0.14)
  blocking collectives: 377 us -> 0 us
  Pallas kernels: 0 us -> 75 us
  waiting for transfers between devices: 68 us -> 0 us
  starting transfers between devices: 59.3 us -> 0 us
  matrix products: 20 us -> 0 us
  local copies, waits for them, and re-layouts: 20.6 us -> 4.4 us
  other arithmetic: 10.2 us -> 0 us
    psum x5 -> x0, blocking collectives: 377 us -> none  [the longest x3 225 us: squares(): return lax.psum(jnp.sum(residual * residual, axis=1), ('hi', 'lo'))]
    pallas_call x0 -> x1, Pallas kernels: none -> 75 us  [per_device(): pl.pallas_call(functools.partial(kernel, dims), out_shape=jax.ShapeDtypeS...]
    ppermute x24 -> x0, waiting for transfers between devices: 68 us -> none  [partner(): return lax.ppermute(block, axis, route)]
    ppermute x24 -> x0, starting transfers between devices: 59.3 us -> none  [partner(): return lax.ppermute(block, axis, route)]
    dot_general x9 -> x0, matrix products: 20 us -> none  [the longest x3 9.2 us: apply_operator(): jnp.einsum('rp,lpc->lrc', halves, bases, preferred_element_type=jnp.float32)]
    scatter x2 -> x0, local copies, waits for them, and re-layouts: 9.39 us -> none  [per_device(): return jnp.zeros_like(solution).at[:, tree_order].set(solution)]
    gather x2 -> x0, local copies, waits for them, and re-layouts: 6.84 us -> none  [per_device(): tree_rhs = jnp.take(right_side, tree_order, axis=1).astype(jnp.float32)]
  transfers between devices with their start and end apart: 24 -> 0, of which waited for: 24 -> 0; matrix products, arithmetic and copies ran while one was open for 0% -> 0% of each run, Pallas kernels for 0% -> 0%
where the time goes in v1:
time: 79.6 us; the launch traced here: 79.4 us
  Pallas kernels  75 us (94%)
  local copies, waits for them, and re-layouts  4.4 us (6%)
    pallas_call x1, Pallas kernels, per_device(): pl.pallas_call(functools.partial(kernel, dims), out_shape=jax.ShapeDtypeS...  75 us
    unnamed x7, local copies, waits for them, and re-layouts  4.4 us

profile of v1, /device:TPU:1, one launch (start us, length us, event | category | flops | bytes accessed | tf_op | source)
XLA Modules:
  0.0 79.4 jit_solution(6262698302629609534)
XLA Ops:
  0.0 0.0 copy-start
  0.0 2.1 %copy-done = bf16[8,1920,128]{2,1,0:T(8,128)(2,1)S(1)} copy-done((bf16[8,1920,128]{2,1,0:T(8,128)(2,1)S(1)}, bf16[8,1920,128]{2,1,0:T(8,128)(2,1)}, u32[]{:S(2)}) %copy-start) | copy-done | bytes 3932184
  2.1 0.0 copy-start.1
  2.1 0.9 %copy-done.1 = bf16[32,1920]{1,0:T(8,128)(2,1)S(1)} copy-done((bf16[32,1920]{1,0:T(8,128)(2,1)S(1)}, bf16[32,1920]{1,0:T(8,128)(2,1)}, u32[]{:S(2)}) %copy-start.1) | copy-done | bytes 122904
  3.0 0.0 copy-start.2
  3.0 0.7 copy-done.2
  3.7 75.0 %tree_cg.1 = f32[32,1920]{1,0:T(8,128)S(1)} custom-call(bf16[32,1920]{1,0:T(8,128)(2,1)S(1)} %copy-done.1, s32[1,1920]{1,0:T(1,128)S(1)} %copy-done.2, bf16[1920,1920]{1,0:T(8,128)(2,1)} %leaf_hbm.1, bf16[8,1920,128]{2,1,0:T(8,128)(2,1)S(1)} %copy-done), custom_call_target="tpu_custom_call" | custom-call | tf_op jit(solution)/shard_map/tree_cg/pallas_call | solution.py:363
  78.7 0.7 copy.6
Async XLA Ops:
  0.0 2.1 %copy-start = (bf16[8,1920,128]{2,1,0:T(8,128)(2,1)S(1)}, bf16[8,1920,128]{2,1,0:T(8,128)(2,1)}, u32[]{:S(2)}) copy-start(bf16[8,1920,128]{2,1,0:T(8,128)(2,1)} %bases_hbm.1) | copy-start | bytes 11796484
  2.1 0.9 %copy-start.1 = (bf16[32,1920]{1,0:T(8,128)(2,1)S(1)}, bf16[32,1920]{1,0:T(8,128)(2,1)}, u32[]{:S(2)}) copy-start(bf16[32,1920]{1,0:T(8,128)(2,1)} %rhs_ref.1) | copy-start | bytes 368644
  3.0 0.7 copy-start.2

commit v2 on v1

v2 whole, which is shorter than its diff:
```python
import functools

import jax
import jax.numpy as jnp
from jax import lax
from jax.experimental import pallas as pl
from jax.experimental.pallas import tpu as pltpu
from jax.sharding import PartitionSpec as P

ITERS = 3
Z_COUNT = 8
VMEM_BYTES = 60 * 1024 * 1024
MESH = pl.DeviceIdType.MESH
F32 = jnp.float32
BF16 = jnp.bfloat16
NN = (((1,), (0,)), ((), ()))
NT = (((1,), (1,)), ((), ()))


def bits(count):
    return count.bit_length() - 1


def spans(total, width):
    return [(low, min(width, total - low)) for low in range(0, total, width)]


def split(value):
    high = value.astype(BF16)
    low = (value - high.astype(F32)).astype(BF16)
    return high, low


def product(left, right, numbers):
    rows = left.shape[0] // 2
    both = lax.dot_general(left, right, numbers, preferred_element_type=F32)
    return both[:rows] + both[rows:]


def row_dot(a, b):
    return jnp.sum(a * b, axis=1, keepdims=True)


def pack_columns(columns):
    count = columns[0].shape[0]
    lane = lax.broadcasted_iota(jnp.int32, (count, 128), 1)
    row = lax.broadcasted_iota(jnp.int32, (count, 128), 0)
    spread = jnp.zeros((count, 128), F32)
    for kind, column in enumerate(columns):
        spread = jnp.where(lane == row + kind * count, column, spread)
    return jnp.sum(spread, axis=0, keepdims=True)


def unpack_column(packed, kind, count):
    lane = lax.broadcasted_iota(jnp.int32, (count, 128), 1)
    row = lax.broadcasted_iota(jnp.int32, (count, 128), 0)
    picked = jnp.where(lane == row + kind * count, packed, 0.0)
    return jnp.sum(picked, axis=1, keepdims=True)


def tree_steps(blocks, first_level, per_level):
    rows = blocks[0].shape[0]
    level_of_row = lax.broadcasted_iota(jnp.int32, (rows, 128), 0) // per_level
    products = jnp.zeros((rows, 128), F32)
    node_sums = []
    current = blocks
    level = first_level
    while len(current) > 1:
        node_sums.append(current)
        pairs = [(current[m], current[m + 1]) for m in range(0, len(current), 2)]
        total = sum(a * b for a, b in pairs)
        products = products + jnp.where(level_of_row == level, total, 0.0)
        current = [a + b for a, b in pairs]
        level += 1
    return node_sums, current[0], products


def fold_levels(products, per_level):
    column = jnp.sum(products, axis=1, keepdims=True)
    total = column[:per_level]
    for low in range(per_level, products.shape[0], per_level):
        total = total + column[low:low + per_level]
    return 2.0 * total


def kernel(dims, rhs_hbm, order_hbm, leaf_hbm, bases_hbm, out_ref, *scratch):
    nz, ny, nh = dims
    (rhs_ref, order_ref, blocks, basis, onehot, halves, sib_f32, sib_halves, residual, direction,
     image, far_dir, near, placed, pending, c_send, c_recv, l_send, l_recv, y_send, y_recv, h_send,
     h_recv, a_send, a_recv, b_send, b_recv, s_send, sy_recv, sh_recv, sz_recv, load_sem, send_sem,
     recv_sem) = scratch
    rhs_count, leaf = residual.shape
    levels = bases_hbm.shape[0]
    own = rhs_count // nz
    zb, yb, hb = bits(nz), bits(ny), bits(nh)
    c_rows = c_send.shape[2]
    h_low = yb * own // 8 * 8
    h_first = yb * own - h_low

    hi = lax.axis_index("hi")
    lo = lax.axis_index("lo")
    z = lax.rem(lo, nz)
    y = lo // nz

    z_steps = sorted(range(1, nz), key=lambda step: -min(step, nz - step))
    y_steps = sorted(range(1, ny), key=lambda step: -min(step, ny - step))
    h_steps = sorted(range(1, nh), key=lambda step: -min(step, nh - step))

    def z_device(step):
        return (hi, y * nz + lax.rem(z + step, nz))

    def y_device(step):
        return (hi, lax.rem(y + step, ny) * nz + z)

    def h_device(step):
        return (lax.rem(hi + step, nh), lo)

    partners = [z_device(step) for step in z_steps]
    partners += [y_device(step) for step in y_steps]
    partners += [h_device(step) for step in h_steps]

    loads = []
    for level in range(levels):
        loads.append(pltpu.make_async_copy(
            bases_hbm.at[level], basis.at[:, pl.ds(128 * level, 128)], load_sem.at[level]))
    loads.append(pltpu.make_async_copy(leaf_hbm, blocks, load_sem.at[levels]))
    loads.insert(0, pltpu.make_async_copy(rhs_hbm, rhs_ref, load_sem.at[levels + 1]))
    loads.insert(0, pltpu.make_async_copy(order_hbm, order_ref, load_sem.at[levels + 2]))
    for load in loads:
        load.start()

    barrier = pltpu.get_barrier_semaphore()
    for partner in partners:
        pl.semaphore_signal(barrier, inc=1, device_id=partner, device_id_type=MESH)

    def send(src, dst, t, phase, partner):
        pltpu.make_async_remote_copy(
            src_ref=src, dst_ref=dst, send_sem=send_sem.at[t, phase],
            recv_sem=recv_sem.at[t, phase], device_id=partner, device_id_type=MESH,
        ).start()

    def await_recv(slots, t, phase):
        pltpu.make_async_copy(slots, slots, recv_sem.at[t, phase]).wait()

    def await_send(slots, t, phase):
        pltpu.make_async_copy(slots, slots, send_sem.at[t, phase]).wait()

    for load in loads[:2]:
        load.wait()
    order_row = order_ref[...]
    for low, width in spans(leaf, 128):
        place = lax.broadcasted_iota(jnp.int32, (width, leaf), 0) + low
        onehot[pl.ds(low, width), :] = jnp.where(place == order_row, 1.0, 0.0).astype(BF16)
    rhs_now = rhs_ref[...]
    for low, width in spans(leaf, 384):
        columns = pl.ds(low, width)
        tree = lax.dot_general(rhs_now, onehot[:, columns], NN, preferred_element_type=F32)
        residual[:, columns] = tree
        high, small = split(tree)
        halves[:, columns] = jnp.concatenate([high, small], axis=0)
    direction[...] = jnp.zeros_like(direction)
    image[...] = jnp.zeros_like(image)
    far_dir[...] = jnp.zeros_like(far_dir)
    placed[...] = jnp.zeros_like(placed)
    out_ref[...] = jnp.zeros_like(out_ref)

    for load in loads[2:levels + 2]:
        load.wait()

    def exchange(t, first, last):
        projected = product(halves[...], basis[...], NN)
        for j in range(nz):
            for level in range(levels):
                target, at = (l_send, level) if level < zb else (c_send, level - zb)
                target[t, j, own * at:own * at + own, :] = (
                    projected[own * j:own * j + own, 128 * level:128 * level + 128])
        if first:
            pl.semaphore_wait(barrier, len(partners))
        for step in z_steps:
            peer = lax.rem(z + step, nz)
            send(c_send.at[t, peer], c_recv.at[t, z], t, 0, z_device(step))
        for step in z_steps:
            peer = lax.rem(z + step, nz)
            send(l_send.at[t, peer], l_recv.at[t, z], t, 1, z_device(step))
        c_recv[t, z] = c_send[t, z]
        l_recv[t, z] = l_send[t, z]
        if first:
            loads[levels + 2].wait()

        rr = jnp.zeros((rhs_count, 1), F32)
        rn = jnp.zeros((rhs_count, 1), F32)
        cross = jnp.zeros((rhs_count, 1), F32)
        for low, width in spans(leaf, 384):
            columns = pl.ds(low, width)
            near_now = product(halves[...], blocks[:, columns], NN)
            near[:, columns] = near_now
            r_now = residual[:, columns]
            rr = rr + row_dot(r_now, r_now)
            rn = rn + row_dot(r_now, near_now)
            if not first:
                cross = cross + row_dot(r_now, image[:, columns] + far_dir[:, columns])
                cross = cross + row_dot(direction[:, columns], near_now)
        packed = pack_columns([rr, rn, cross])

        lane = lax.broadcasted_iota(jnp.int32, (own, 128), 1)
        row = lax.broadcasted_iota(jnp.int32, (own, 128), 0)
        mine = lane == row + rhs_count + z * own

        def add_products(packed, products):
            placed_dots = jnp.where(mine, fold_levels(products, own), 0.0)
            return packed + jnp.sum(placed_dots, axis=0, keepdims=True)

        await_recv(c_recv.at[t, pl.ds(0, nz - 1)], t, 0)
        total = c_recv[t, 0]
        for j in range(1, nz):
            total = total + c_recv[t, j]
        y_send[t] = total
        for step in y_steps:
            send(y_send.at[t], y_recv.at[t, y], t, 2, y_device(step))
        y_recv[t, y] = total

        await_recv(l_recv.at[t, pl.ds(0, nz - 1)], t, 1)
        node_sums, _, products = tree_steps([l_recv[t, j] for j in range(nz)], 0, own)
        packed = add_products(packed, products)
        s_send[t, 0] = packed
        for step in y_steps:
            send(s_send.at[t, 0], sy_recv.at[t, y], t, 3, y_device(step))
        sy_recv[t, y] = packed
        if not last:
            for j in range(nz):
                for level in range(zb):
                    rows = slice(own * level, own * level + own)
                    a_send[t, j, rows] = node_sums[level][(j >> level) ^ 1][rows]
            for step in z_steps:
                peer = lax.rem(z + step, nz)
                send(a_send.at[t, peer], a_recv.at[t, z], t, 4, z_device(step))
            a_recv[t, z] = a_send[t, z]
        if not first:
            place_chunk(0)

        await_recv(y_recv.at[t, pl.ds(0, ny - 1)], t, 2)
        _, total, products = tree_steps([y_recv[t, j] for j in range(ny)], 0, own)
        h_send[t] = total[h_low:]
        for step in h_steps:
            send(h_send.at[t], h_recv.at[t, hi], t, 5, h_device(step))
        h_recv[t, hi] = h_send[t]
        await_recv(sy_recv.at[t, pl.ds(0, ny - 1)], t, 3)
        packed = sum(sy_recv[t, j] for j in range(ny))
        packed = add_products(packed, products)
        s_send[t, 1] = packed
        for step in h_steps:
            send(s_send.at[t, 1], sh_recv.at[t, hi], t, 6, h_device(step))
        sh_recv[t, hi] = packed
        if not last:
            for level in range(yb):
                rows = slice(own * level, own * level + own)
                first_node = ((y >> level) + 1 - 2 * lax.rem(y >> level, 2)) << level
                found = y_recv[t, first_node, rows]
                for extra in range(1, 1 << level):
                    found = found + y_recv[t, first_node + extra, rows]
                b_send[t, rows] = found
        if not first:
            place_chunk(1)

        await_recv(h_recv.at[t, pl.ds(0, nh - 1)], t, 5)
        if not last:
            for level in range(hb):
                from_rows = slice(h_first + own * level, h_first + own * level + own)
                first_node = ((hi >> level) + 1 - 2 * lax.rem(hi >> level, 2)) << level
                found = h_recv[t, first_node, from_rows]
                for extra in range(1, 1 << level):
                    found = found + h_recv[t, first_node + extra, from_rows]
                b_send[t, own * (yb + level):own * (yb + level) + own] = found
            for step in z_steps:
                send(b_send.at[t], b_recv.at[t, z], t, 7, z_device(step))
            b_recv[t, z] = b_send[t]
        _, _, products = tree_steps([h_recv[t, j] for j in range(nh)], h_first // own, own)
        await_recv(sh_recv.at[t, pl.ds(0, nh - 1)], t, 6)
        packed = sum(sh_recv[t, j] for j in range(nh))
        packed = add_products(packed, products)
        s_send[t, 2] = packed
        for step in z_steps:
            send(s_send.at[t, 2], sz_recv.at[t, z], t, 8, z_device(step))
        sz_recv[t, z] = packed
        if not first:
            place_chunk(2)

        if not last:
            await_recv(a_recv.at[t, pl.ds(0, nz - 1)], t, 4)
            await_recv(b_recv.at[t, pl.ds(0, nz - 1)], t, 7)
            for j in range(nz):
                for level in range(levels):
                    source, at = (a_recv, level) if level < zb else (b_recv, level - zb)
                    sib_f32[own * j:own * j + own, 128 * level:128 * level + 128] = (
                        source[t, j, own * at:own * at + own, :])
            high, small = split(sib_f32[...])
            sib_halves[...] = jnp.concatenate([high, small], axis=0)
        await_recv(sz_recv.at[t, pl.ds(0, nz - 1)], t, 8)
        packed = sum(sz_recv[t, j] for j in range(nz))
        return [unpack_column(packed, kind, rhs_count) for kind in range(3)]

    third = leaf // 3

    def place_chunk(number):
        for low, width in spans(third, 640):
            rows = pl.ds(number * third + low, width)
            pending[:, rows] = product(halves[...], onehot[rows, :], NT)

    rr_old = jnp.ones((rhs_count, 1), F32)
    curvature = jnp.zeros((rhs_count, 1), F32)
    for t in range(ITERS):
        first, last = t == 0, t == ITERS - 1
        rr, rn, cross = exchange(t, first, last)
        beta = jnp.zeros_like(rr) if first else rr / rr_old
        curvature = rn + beta * cross + beta * beta * curvature
        alpha = rr / curvature
        rr_old = rr
        here = rhs_now.astype(F32) if first else pending[...]
        place_now = here + beta * placed[...]
        placed[...] = place_now
        out_ref[...] = out_ref[...] + alpha * place_now
        if last:
            break
        for low, width in spans(leaf, 384):
            columns = pl.ds(low, width)
            far = product(sib_halves[...], basis[columns, :], NT)
            far_now = far + beta * far_dir[:, columns]
            far_dir[:, columns] = far_now
            image_now = near[:, columns] + far + beta * image[:, columns]
            image[:, columns] = image_now
            r_now = residual[:, columns]
            direction[:, columns] = r_now + beta * direction[:, columns]
            r_next = r_now - alpha * image_now
            residual[:, columns] = r_next
            high, small = split(r_next)
            halves[:, columns] = jnp.concatenate([high, small], axis=0)

    for t in range(ITERS):
        await_send(c_recv.at[t, pl.ds(0, nz - 1)], t, 0)
        await_send(l_recv.at[t, pl.ds(0, nz - 1)], t, 1)
        await_send(y_recv.at[t, pl.ds(0, ny - 1)], t, 2)
        await_send(sy_recv.at[t, pl.ds(0, ny - 1)], t, 3)
        await_send(h_recv.at[t, pl.ds(0, nh - 1)], t, 5)
        await_send(sh_recv.at[t, pl.ds(0, nh - 1)], t, 6)
        await_send(sz_recv.at[t, pl.ds(0, nz - 1)], t, 8)
        if t < ITERS - 1:
            await_send(a_recv.at[t, pl.ds(0, nz - 1)], t, 4)
            await_send(b_recv.at[t, pl.ds(0, nz - 1)], t, 7)


def per_device(dims, right_side, point_order, leaf_blocks, bases):
    nz, ny, nh = dims
    rhs_count, leaf = right_side.shape
    levels = bases.shape[0]
    own = rhs_count // nz
    yb = bits(ny)
    l_rows = bits(nz) * own
    c_rows = levels * own - l_rows
    h_rows = c_rows - yb * own // 8 * 8
    vector = pltpu.VMEM((rhs_count, leaf), F32)

    def buffer(*shape):
        return pltpu.VMEM((ITERS, *shape, 128), F32)

    scratch = [
        pltpu.VMEM((rhs_count, leaf), BF16),
        pltpu.VMEM((1, leaf), jnp.int32),
        pltpu.VMEM((leaf, leaf), BF16),
        pltpu.VMEM((leaf, 128 * levels), BF16),
        pltpu.VMEM((leaf, leaf), BF16),
        pltpu.VMEM((2 * rhs_count, leaf), BF16),
        pltpu.VMEM((rhs_count, 128 * levels), F32),
        pltpu.VMEM((2 * rhs_count, 128 * levels), BF16),
        vector, vector, vector, vector, vector, vector, vector,
        buffer(nz, c_rows), buffer(nz, c_rows),
        buffer(nz, l_rows), buffer(nz, l_rows),
        buffer(c_rows), buffer(ny, c_rows),
        buffer(h_rows), buffer(nh, h_rows),
        buffer(nz, l_rows), buffer(nz, l_rows),
        buffer(c_rows), buffer(nz, c_rows),
        buffer(3, 1), buffer(ny, 1), buffer(nh, 1), buffer(nz, 1),
        pltpu.SemaphoreType.DMA((levels + 3,)),
        pltpu.SemaphoreType.DMA((ITERS, 9)),
        pltpu.SemaphoreType.DMA((ITERS, 9)),
    ]
    return pl.pallas_call(
        functools.partial(kernel, dims),
        out_shape=jax.ShapeDtypeStruct((rhs_count, leaf), F32),
        in_specs=[
            pl.BlockSpec(memory_space=pl.ANY),
            pl.BlockSpec(memory_space=pl.ANY),
            pl.BlockSpec(memory_space=pl.ANY),
            pl.BlockSpec(memory_space=pl.ANY),
        ],
        out_specs=pl.BlockSpec(memory_space=pltpu.VMEM),
        scratch_shapes=scratch,
        compiler_params=pltpu.CompilerParams(
            collective_id=0, has_side_effects=True, vmem_limit_bytes=VMEM_BYTES
        ),
        name="tree_cg",
    )(right_side, point_order, leaf_blocks, bases)


def solution(mesh):
    dims = (Z_COUNT, mesh.shape["lo"] // Z_COUNT, mesh.shape["hi"])
    in_specs = (
        P(None, ("hi", "lo")),
        P(("hi", "lo"), None),
        P(("hi", "lo"), None),
        P(None, ("hi", "lo"), None),
    )
    return jax.shard_map(
        functools.partial(per_device, dims), mesh=mesh, in_specs=in_specs,
        out_specs=P(None, ("hi", "lo")), check_vma=False
    )
```

time: 79.6 us -> 69 us (0.87)
  Pallas kernels: 75 us -> 67.3 us
  local copies, waits for them, and re-layouts: 4.4 us -> 1.65 us
    pallas_call x1, Pallas kernels: 75 us -> 67.3 us  [per_device(): pl.pallas_call(functools.partial(kernel, dims), out_shape=jax.ShapeDtypeS...]
    unnamed x7 -> x1, local copies, waits for them, and re-layouts: 4.4 us -> 1.65 us
where the time goes in v2:
time: 69 us; the launch traced here: 68.9 us
  Pallas kernels  67.3 us (98%)
  local copies, waits for them, and re-layouts  1.65 us (2%)
    pallas_call x1, Pallas kernels, per_device(): pl.pallas_call(functools.partial(kernel, dims), out_shape=jax.ShapeDtypeS...  67.3 us
    unnamed x1, local copies, waits for them, and re-layouts  1.65 us

profile of v2, /device:TPU:1, one launch (start us, length us, event | category | flops | bytes accessed | tf_op | source)
XLA Modules:
  0.0 68.9 jit_solution(7009627491090987301)
XLA Ops:
  0.0 67.3 %tree_cg.1 = f32[32,1920]{1,0:T(8,128)} custom-call(bf16[32,1920]{1,0:T(8,128)(2,1)} %rhs_hbm.1, s32[1,1920]{1,0:T(1,128)} %order_hbm.1, bf16[1920,1920]{1,0:T(8,128)(2,1)} %leaf_hbm.1, bf16[8,1920,128]{2,1,0:T(8,128)(2,1)} %bases_hbm.1), custom_call_target="tpu_custom_call" | custom-call | tf_op jit(solution)/shard_map/tree_cg/pallas_call | solution.py:386
  67.3 1.7 %copy.6 = f32[32,1920]{1,0:T(8,128)} copy(f32[32,1920]{1,0:T(8,128)} %tree_cg.1) | data formatting | bytes 491520

commit v3 on v2

v3 whole, which is shorter than its diff:
```python
import functools

import jax
import jax.numpy as jnp
from jax import lax
from jax.experimental import pallas as pl
from jax.experimental.pallas import tpu as pltpu
from jax.sharding import PartitionSpec as P

ITERS = 3
Z_COUNT = 8
VMEM_BYTES = 60 * 1024 * 1024
MESH = pl.DeviceIdType.MESH
F32 = jnp.float32
BF16 = jnp.bfloat16
NN = (((1,), (0,)), ((), ()))
NT = (((1,), (1,)), ((), ()))


def bits(count):
    return count.bit_length() - 1


def spans(total, width):
    return [(low, min(width, total - low)) for low in range(0, total, width)]


def split(value):
    high = value.astype(BF16)
    low = (value - high.astype(F32)).astype(BF16)
    return high, low


def product(left, right, numbers):
    rows = left.shape[0] // 2
    both = lax.dot_general(left, right, numbers, preferred_element_type=F32)
    return both[:rows] + both[rows:]


def row_dot(a, b):
    return jnp.sum(a * b, axis=1, keepdims=True)


def pack_columns(columns):
    count = columns[0].shape[0]
    lane = lax.broadcasted_iota(jnp.int32, (count, 128), 1)
    row = lax.broadcasted_iota(jnp.int32, (count, 128), 0)
    spread = jnp.zeros((count, 128), F32)
    for kind, column in enumerate(columns):
        spread = jnp.where(lane == row + kind * count, column, spread)
    return jnp.sum(spread, axis=0, keepdims=True)


def unpack_column(packed, first, count):
    lane = lax.broadcasted_iota(jnp.int32, (count, 128), 1)
    row = lax.broadcasted_iota(jnp.int32, (count, 128), 0)
    picked = jnp.where(lane == row + first, packed, 0.0)
    return jnp.sum(picked, axis=1, keepdims=True)


def next_scalars(sums, rr_old, curvature):
    rr, rn, cross = sums
    if rr_old is None:
        beta = jnp.zeros_like(rr)
        curvature = rn
    else:
        beta = rr / rr_old
        curvature = rn + beta * cross + beta * beta * curvature
    return rr / curvature, beta, rr, curvature


def tree_steps(blocks, first_level, per_level):
    rows = blocks[0].shape[0]
    level_of_row = lax.broadcasted_iota(jnp.int32, (rows, 128), 0) // per_level
    products = jnp.zeros((rows, 128), F32)
    node_sums = []
    current = blocks
    level = first_level
    while len(current) > 1:
        node_sums.append(current)
        pairs = [(current[m], current[m + 1]) for m in range(0, len(current), 2)]
        total = sum(a * b for a, b in pairs)
        products = products + jnp.where(level_of_row == level, 2.0 * total, 0.0)
        current = [a + b for a, b in pairs]
        level += 1
    return node_sums, current[0], products


def fold_levels(products, per_level):
    column = jnp.sum(products, axis=1, keepdims=True)
    total = column[:per_level]
    for low in range(per_level, products.shape[0], per_level):
        total = total + column[low:low + per_level]
    return total


def kernel(dims, rhs_hbm, order_hbm, leaf_hbm, bases_hbm, out_ref, *scratch):
    nz, ny, nh = dims
    (rhs_ref, order_ref, blocks, basis, onehot, halves, sib_f32, sib_halves, residual, direction,
     image, far_dir, near, placed, pending, c_send, c_recv, l_send, l_recv, y_send, y_recv, h_send,
     h_recv, a_send, a_recv, b_send, b_recv, x_send, x_recv, s_send, sx_recv, sy_recv, sh_recv,
     sz_recv, l_now, l_image, c_now, c_image, far, sent, load_sem, send_sem, recv_sem) = scratch
    rhs_count, leaf = residual.shape
    levels = bases_hbm.shape[0]
    own = rhs_count // nz
    zb, yb, hb = bits(nz), bits(ny), bits(nh)
    c_rows = c_send.shape[2]
    h_low = yb * own // 8 * 8
    h_first = yb * own - h_low

    hi = lax.axis_index("hi")
    lo = lax.axis_index("lo")
    z = lax.rem(lo, nz)
    y = lo // nz

    z_steps = sorted(range(1, nz), key=lambda step: -min(step, nz - step))
    y_steps = sorted(range(1, ny), key=lambda step: -min(step, ny - step))
    h_steps = sorted(range(1, nh), key=lambda step: -min(step, nh - step))

    def z_device(step):
        return (hi, y * nz + lax.rem(z + step, nz))

    def y_device(step):
        return (hi, lax.rem(y + step, ny) * nz + z)

    def h_device(step):
        return (lax.rem(hi + step, nh), lo)

    upper = hi * ny + y
    masks = sorted(range(1, nh * ny), key=lambda mask: -mask.bit_count())

    def x_device(mask):
        other = upper
        for bit in range(bits(nh * ny)):
            if mask >> bit & 1:
                other = other + (1 - 2 * lax.rem(upper // (1 << bit), 2)) * (1 << bit)
        return (other // ny, lax.rem(other, ny) * nz + z)

    partners = [z_device(step) for step in z_steps]
    partners += [x_device(mask) for mask in masks]

    loads = []
    for level in range(levels):
        loads.append(pltpu.make_async_copy(
            bases_hbm.at[level], basis.at[:, pl.ds(128 * level, 128)], load_sem.at[level]))
    loads.append(pltpu.make_async_copy(leaf_hbm, blocks, load_sem.at[levels]))
    loads.insert(0, pltpu.make_async_copy(rhs_hbm, rhs_ref, load_sem.at[levels + 1]))
    loads.insert(0, pltpu.make_async_copy(order_hbm, order_ref, load_sem.at[levels + 2]))
    for load in loads:
        load.start()

    barrier = pltpu.get_barrier_semaphore()
    for partner in partners:
        pl.semaphore_signal(barrier, inc=1, device_id=partner, device_id_type=MESH)

    def send(src, dst, t, phase, partner):
        pltpu.make_async_remote_copy(
            src_ref=src, dst_ref=dst, send_sem=send_sem.at[t, phase],
            recv_sem=recv_sem.at[t, phase], device_id=partner, device_id_type=MESH,
        ).start()

    def await_recv(slots, t, phase):
        pltpu.make_async_copy(slots, slots, recv_sem.at[t, phase]).wait()

    def await_send(slots, t, phase):
        pltpu.make_async_copy(slots, slots, send_sem.at[t, phase]).wait()

    for load in loads[:2]:
        load.wait()
    order_row = order_ref[...]
    for low, width in spans(leaf, 128):
        place = lax.broadcasted_iota(jnp.int32, (width, leaf), 0) + low
        onehot[pl.ds(low, width), :] = jnp.where(place == order_row, 1.0, 0.0).astype(BF16)
    rhs_now = rhs_ref[...]
    for low, width in spans(leaf, 384):
        columns = pl.ds(low, width)
        tree = lax.dot_general(rhs_now, onehot[:, columns], NN, preferred_element_type=F32)
        residual[:, columns] = tree
        high, small = split(tree)
        halves[:, columns] = jnp.concatenate([high, small], axis=0)
    for load in loads[2:levels + 2]:
        load.wait()

    lane = lax.broadcasted_iota(jnp.int32, (own, 128), 1)
    row = lax.broadcasted_iota(jnp.int32, (own, 128), 0)
    mine = lane == row + rhs_count + z * own

    def add_dots(packed, products):
        spread = jnp.where(mine, fold_levels(products, own), 0.0)
        return packed + jnp.sum(spread, axis=0, keepdims=True)

    def send_projections(t, vector):
        projected = product(vector[...], basis[...], NN)
        for j in range(nz):
            for level in range(levels):
                target, at = (l_send, level) if level < zb else (c_send, level - zb)
                target[t, j, own * at:own * at + own, :] = (
                    projected[own * j:own * j + own, 128 * level:128 * level + 128])
        if t == 0:
            pl.semaphore_wait(barrier, len(partners))
        for step in z_steps:
            peer = lax.rem(z + step, nz)
            send(c_send.at[t, peer], c_recv.at[t, z], t, 0, z_device(step))
        for step in z_steps:
            peer = lax.rem(z + step, nz)
            send(l_send.at[t, peer], l_recv.at[t, z], t, 1, z_device(step))
        c_recv[t, z] = c_send[t, z]
        l_recv[t, z] = l_send[t, z]

    def near_and_dots(first):
        rr = jnp.zeros((rhs_count, 1), F32)
        rn = jnp.zeros((rhs_count, 1), F32)
        cross = jnp.zeros((rhs_count, 1), F32)
        for low, width in spans(leaf, 384):
            columns = pl.ds(low, width)
            near_now = product(halves[...], blocks[:, columns], NN)
            near[:, columns] = near_now
            r_now = residual[:, columns]
            rr = rr + row_dot(r_now, r_now)
            rn = rn + row_dot(r_now, near_now)
            if not first:
                cross = cross + row_dot(r_now, image[:, columns] + far_dir[:, columns])
                cross = cross + row_dot(direction[:, columns], near_now)
        return pack_columns([rr, rn, cross])

    def upper_sums(t, owned):
        await_recv(c_recv.at[t, pl.ds(0, nz - 1)], t, 0)
        total = c_recv[t, 0]
        for j in range(1, nz):
            total = total + c_recv[t, j]
        if t > 0:
            alpha, beta = (jnp.concatenate([v] * (c_rows // own), axis=0) for v in owned)
            if t > 1:
                total = total + beta * c_image[...]
            c_image[...] = total
            total = c_now[...] - alpha * total
        c_now[...] = total
        return total

    def lower_sums(t, owned):
        await_recv(l_recv.at[t, pl.ds(0, nz - 1)], t, 1)
        found = []
        for j in range(nz):
            block = l_recv[t, j]
            if t > 0:
                alpha, beta = (jnp.concatenate([v] * zb, axis=0) for v in owned)
                if t > 1:
                    block = block + beta * l_image[j]
                l_image[j] = block
                block = l_now[j] - alpha * block
            l_now[j] = block
            found.append(block)
        node_sums, _, products = tree_steps(found, 0, own)
        return node_sums, products

    def siblings(t, owned):
        if t == 0:
            loads[levels + 2].wait()
        packed = near_and_dots(t == 0)
        total = upper_sums(t, owned)
        for bit in range(yb + hb):
            x_send[t, bit] = total[own * bit:own * bit + own]
        for mask in masks:
            bit = mask.bit_length() - 1
            send(x_send.at[t, bit], x_recv.at[t, mask], t, 9, x_device(mask))
        node_sums, products = lower_sums(t, owned)
        packed = add_dots(packed, products)
        for j in range(nz):
            for level in range(zb):
                rows = slice(own * level, own * level + own)
                a_send[t, j, rows] = node_sums[level][(j >> level) ^ 1][rows]
        for step in z_steps:
            peer = lax.rem(z + step, nz)
            send(a_send.at[t, peer], a_recv.at[t, z], t, 4, z_device(step))
        a_recv[t, z] = a_send[t, z]

        await_recv(x_recv.at[t, pl.ds(1, nh * ny - 1)], t, 9)
        for bit in range(yb + hb):
            b_send[t, own * bit:own * bit + own] = sum(
                x_recv[t, mask] for mask in range(1 << bit, 2 << bit))
        for step in z_steps:
            send(b_send.at[t], b_recv.at[t, z], t, 7, z_device(step))
        b_recv[t, z] = b_send[t]
        packed = add_dots(packed, total * b_send[t])
        s_send[t, 0] = packed
        for mask in masks:
            send(s_send.at[t, 0], sx_recv.at[t, mask], t, 10, x_device(mask))
        if t > 0:
            for number in range(3):
                place_chunk(number)
        await_recv(sx_recv.at[t, pl.ds(1, nh * ny - 1)], t, 10)
        for mask in range(1, nh * ny):
            packed = packed + sx_recv[t, mask]
        s_send[t, 1] = packed
        for step in z_steps:
            send(s_send.at[t, 1], sz_recv.at[t, z], t, 8, z_device(step))
        sz_recv[t, z] = packed

        await_recv(a_recv.at[t, pl.ds(0, nz - 1)], t, 4)
        await_recv(b_recv.at[t, pl.ds(0, nz - 1)], t, 7)
        for j in range(nz):
            for level in range(levels):
                source, at = (a_recv, level) if level < zb else (b_recv, level - zb)
                sib_f32[own * j:own * j + own, 128 * level:128 * level + 128] = (
                    source[t, j, own * at:own * at + own, :])
        high, small = split(sib_f32[...])
        sib_halves[...] = jnp.concatenate([high, small], axis=0)
        for low, width in spans(leaf, 384):
            columns = pl.ds(low, width)
            far_now = product(sib_halves[...], basis[columns, :], NT)
            far[:, columns] = far_now
            high, small = split(near[:, columns] + far_now)
            sent[:, columns] = jnp.concatenate([high, small], axis=0)

    def finish(t, owned):
        packed = near_and_dots(False)
        total = upper_sums(t, owned)
        y_send[...] = total
        for step in y_steps:
            send(y_send, y_recv.at[y], t, 2, y_device(step))
        y_recv[y] = total
        _, products = lower_sums(t, owned)
        packed = add_dots(packed, products)
        s_send[t, 0] = packed
        for step in y_steps:
            send(s_send.at[t, 0], sy_recv.at[y], t, 3, y_device(step))
        sy_recv[y] = packed
        place_chunk(0)

        await_recv(y_recv.at[pl.ds(0, ny - 1)], t, 2)
        _, total, products = tree_steps([y_recv[j] for j in range(ny)], 0, own)
        h_send[...] = total[h_low:]
        for step in h_steps:
            send(h_send, h_recv.at[hi], t, 5, h_device(step))
        h_recv[hi] = total[h_low:]
        await_recv(sy_recv.at[pl.ds(0, ny - 1)], t, 3)
        packed = add_dots(sum(sy_recv[j] for j in range(ny)), products)
        s_send[t, 1] = packed
        for step in h_steps:
            send(s_send.at[t, 1], sh_recv.at[hi], t, 6, h_device(step))
        sh_recv[hi] = packed
        place_chunk(1)

        await_recv(h_recv.at[pl.ds(0, nh - 1)], t, 5)
        _, _, products = tree_steps([h_recv[j] for j in range(nh)], h_first // own, own)
        await_recv(sh_recv.at[pl.ds(0, nh - 1)], t, 6)
        packed = add_dots(sum(sh_recv[j] for j in range(nh)), products)
        s_send[t, 2] = packed
        for step in z_steps:
            send(s_send.at[t, 2], sz_recv.at[t, z], t, 8, z_device(step))
        sz_recv[t, z] = packed
        place_chunk(2)

    def total_scalars(t):
        await_recv(sz_recv.at[t, pl.ds(0, nz - 1)], t, 8)
        return sum(sz_recv[t, j] for j in range(nz))

    third = leaf // 3

    def place_chunk(number):
        for low, width in spans(third, 640):
            rows = pl.ds(number * third + low, width)
            pending[:, rows] = product(halves[...], onehot[rows, :], NT)

    state, owned_state, owned = (None, None), (None, None), None
    send_projections(0, halves)
    for t in range(ITERS):
        if t < ITERS - 1:
            siblings(t, owned)
            send_projections(t + 1, sent)
        else:
            finish(t, owned)
        packed = total_scalars(t)
        sums = [unpack_column(packed, kind * rhs_count, rhs_count) for kind in range(3)]
        alpha, beta, *state = next_scalars(sums, *state)
        here = rhs_now.astype(F32) if t == 0 else pending[...] + beta * placed[...]
        if t == ITERS - 1:
            out_ref[...] = out_ref[...] + alpha * here
            break
        sums = [unpack_column(packed, kind * rhs_count + z * own, own) for kind in range(3)]
        *owned, rr_owned, curvature = next_scalars(sums, *owned_state)
        owned_state = rr_owned, curvature
        for low, width in spans(leaf, 384):
            columns = pl.ds(low, width)
            r_now = residual[:, columns]
            far_now = far[:, columns]
            image_now = near[:, columns] + far_now
            direction_now = r_now
            if t > 0:
                far_now = far_now + beta * far_dir[:, columns]
                image_now = image_now + beta * image[:, columns]
                direction_now = direction_now + beta * direction[:, columns]
            far_dir[:, columns] = far_now
            image[:, columns] = image_now
            direction[:, columns] = direction_now
            r_next = r_now - alpha * image_now
            residual[:, columns] = r_next
            high, small = split(r_next)
            halves[:, columns] = jnp.concatenate([high, small], axis=0)
        placed[...] = here
        out_ref[...] = alpha * here if t == 0 else out_ref[...] + alpha * here

    for t in range(ITERS):
        await_send(c_recv.at[t, pl.ds(0, nz - 1)], t, 0)
        await_send(l_recv.at[t, pl.ds(0, nz - 1)], t, 1)
        await_send(sz_recv.at[t, pl.ds(0, nz - 1)], t, 8)
        if t < ITERS - 1:
            await_send(x_recv.at[t, pl.ds(1, nh * ny - 1)], t, 9)
            await_send(sx_recv.at[t, pl.ds(1, nh * ny - 1)], t, 10)
            await_send(a_recv.at[t, pl.ds(0, nz - 1)], t, 4)
            await_send(b_recv.at[t, pl.ds(0, nz - 1)], t, 7)
        else:
            await_send(y_recv.at[pl.ds(0, ny - 1)], t, 2)
            await_send(sy_recv.at[pl.ds(0, ny - 1)], t, 3)
            await_send(h_recv.at[pl.ds(0, nh - 1)], t, 5)
            await_send(sh_recv.at[pl.ds(0, nh - 1)], t, 6)


def per_device(dims, right_side, point_order, leaf_blocks, bases):
    nz, ny, nh = dims
    rhs_count, leaf = right_side.shape
    levels = bases.shape[0]
    own = rhs_count // nz
    yb = bits(ny)
    l_rows = bits(nz) * own
    c_rows = levels * own - l_rows
    h_rows = c_rows - yb * own // 8 * 8
    vector = pltpu.VMEM((rhs_count, leaf), F32)

    def buffer(*shape):
        return pltpu.VMEM((ITERS, *shape, 128), F32)

    def once(*shape):
        return pltpu.VMEM((*shape, 128), F32)

    scratch = [
        pltpu.VMEM((rhs_count, leaf), BF16),
        pltpu.VMEM((1, leaf), jnp.int32),
        pltpu.VMEM((leaf, leaf), BF16),
        pltpu.VMEM((leaf, 128 * levels), BF16),
        pltpu.VMEM((leaf, leaf), BF16),
        pltpu.VMEM((2 * rhs_count, leaf), BF16),
        pltpu.VMEM((rhs_count, 128 * levels), F32),
        pltpu.VMEM((2 * rhs_count, 128 * levels), BF16),
        vector, vector, vector, vector, vector, vector, vector,
        buffer(nz, c_rows), buffer(nz, c_rows),
        buffer(nz, l_rows), buffer(nz, l_rows),
        once(c_rows), once(ny, c_rows),
        once(h_rows), once(nh, h_rows),
        buffer(nz, l_rows), buffer(nz, l_rows),
        buffer(c_rows), buffer(nz, c_rows),
        buffer(levels - bits(nz), own), buffer(nh * ny, own),
        buffer(3, 1), buffer(nh * ny, 1), once(ny, 1), once(nh, 1), buffer(nz, 1),
        once(nz, l_rows), once(nz, l_rows), once(c_rows), once(c_rows),
        vector, pltpu.VMEM((2 * rhs_count, leaf), BF16),
        pltpu.SemaphoreType.DMA((levels + 3,)),
        pltpu.SemaphoreType.DMA((ITERS, 11)),
        pltpu.SemaphoreType.DMA((ITERS, 11)),
    ]
    return pl.pallas_call(
        functools.partial(kernel, dims),
        out_shape=jax.ShapeDtypeStruct((rhs_count, leaf), F32),
        in_specs=[
            pl.BlockSpec(memory_space=pl.ANY),
            pl.BlockSpec(memory_space=pl.ANY),
            pl.BlockSpec(memory_space=pl.ANY),
            pl.BlockSpec(memory_space=pl.ANY),
        ],
        out_specs=pl.BlockSpec(memory_space=pltpu.VMEM),
        scratch_shapes=scratch,
        compiler_params=pltpu.CompilerParams(
            collective_id=0, has_side_effects=True, vmem_limit_bytes=VMEM_BYTES
        ),
        name="tree_cg",
    )(right_side, point_order, leaf_blocks, bases)


def solution(mesh):
    dims = (Z_COUNT, mesh.shape["lo"] // Z_COUNT, mesh.shape["hi"])
    in_specs = (
        P(None, ("hi", "lo")),
        P(("hi", "lo"), None),
        P(("hi", "lo"), None),
        P(None, ("hi", "lo"), None),
    )
    return jax.shard_map(
        functools.partial(per_device, dims), mesh=mesh, in_specs=in_specs,
        out_specs=P(None, ("hi", "lo")), check_vma=False
    )
```

time: 69 us -> 64.5 us (0.935)
  Pallas kernels: 67.3 us -> 62.8 us
    pallas_call x1, Pallas kernels: 67.3 us -> 62.8 us  [per_device(): pl.pallas_call(functools.partial(kernel, dims), out_shape=jax.ShapeDtypeS...]
where the time goes in v3:
time: 64.5 us; the launch traced here: 64.4 us
  Pallas kernels  62.8 us (97%)
  local copies, waits for them, and re-layouts  1.65 us (3%)
    pallas_call x1, Pallas kernels, per_device(): pl.pallas_call(functools.partial(kernel, dims), out_shape=jax.ShapeDtypeS...  62.8 us
    unnamed x1, local copies, waits for them, and re-layouts  1.65 us

profile of v3, /device:TPU:1, one launch (start us, length us, event | category | flops | bytes accessed | tf_op | source)
XLA Modules:
  0.0 64.4 jit_solution(1776632771060106552)
XLA Ops:
  0.0 62.8 %tree_cg.1 = f32[32,1920]{1,0:T(8,128)} custom-call(bf16[32,1920]{1,0:T(8,128)(2,1)} %rhs_hbm.1, s32[1,1920]{1,0:T(1,128)} %order_hbm.1, bf16[1920,1920]{1,0:T(8,128)(2,1)} %leaf_hbm.1, bf16[8,1920,128]{2,1,0:T(8,128)(2,1)} %bases_hbm.1), custom_call_target="tpu_custom_call" | custom-call | tf_op jit(solution)/shard_map/tree_cg/pallas_call | solution.py:460
  62.8 1.7 %copy.6 = f32[32,1920]{1,0:T(8,128)} copy(f32[32,1920]{1,0:T(8,128)} %tree_cg.1) | data formatting | bytes 491520

commit v4 on v3

--- a/solution.py
+++ b/solution.py
@@ -96,7 +96,7 @@
 
 def kernel(dims, rhs_hbm, order_hbm, leaf_hbm, bases_hbm, out_ref, *scratch):
     nz, ny, nh = dims
-    (rhs_ref, order_ref, blocks, basis, onehot, halves, sib_f32, sib_halves, residual, direction,
+    (rhs_ref, order_ref, blocks, basis, basis_t, onehot, halves, sib_f32, sib_halves, residual, direction,
      image, far_dir, near, placed, pending, c_send, c_recv, l_send, l_recv, y_send, y_recv, h_send,
      h_recv, a_send, a_recv, b_send, b_recv, x_send, x_recv, s_send, sx_recv, sy_recv, sh_recv,
      sz_recv, l_now, l_image, c_now, c_image, far, sent, load_sem, send_sem, recv_sem) = scratch
@@ -127,7 +127,8 @@
         return (lax.rem(hi + step, nh), lo)
 
     upper = hi * ny + y
-    masks = sorted(range(1, nh * ny), key=lambda mask: -mask.bit_count())
+    masks = sorted(range(1, nh * ny), key=lambda mask: -(
+        2 * (0, 1, 2, 1)[mask % ny] + 2 * (0, 1, 2, 1)[mask // ny // 2] + mask // ny % 2))
 
     def x_device(mask):
         other = upper
@@ -138,6 +139,10 @@
 
     partners = [z_device(step) for step in z_steps]
     partners += [x_device(mask) for mask in masks]
+
+    barrier = pltpu.get_barrier_semaphore()
+    for partner in partners:
+        pl.semaphore_signal(barrier, inc=1, device_id=partner, device_id_type=MESH)
 
     loads = []
     for level in range(levels):
@@ -148,10 +153,6 @@
     loads.insert(0, pltpu.make_async_copy(order_hbm, order_ref, load_sem.at[levels + 2]))
     for load in loads:
         load.start()
-
-    barrier = pltpu.get_barrier_semaphore()
-    for partner in partners:
-        pl.semaphore_signal(barrier, inc=1, device_id=partner, device_id_type=MESH)
 
     def send(src, dst, t, phase, partner):
         pltpu.make_async_remote_copy(
@@ -190,20 +191,18 @@
         return packed + jnp.sum(spread, axis=0, keepdims=True)
 
     def send_projections(t, vector):
-        projected = product(vector[...], basis[...], NN)
-        for j in range(nz):
-            for level in range(levels):
-                target, at = (l_send, level) if level < zb else (c_send, level - zb)
-                target[t, j, own * at:own * at + own, :] = (
-                    projected[own * j:own * j + own, 128 * level:128 * level + 128])
-        if t == 0:
-            pl.semaphore_wait(barrier, len(partners))
-        for step in z_steps:
-            peer = lax.rem(z + step, nz)
-            send(c_send.at[t, peer], c_recv.at[t, z], t, 0, z_device(step))
-        for step in z_steps:
-            peer = lax.rem(z + step, nz)
-            send(l_send.at[t, peer], l_recv.at[t, z], t, 1, z_device(step))
+        parts = ((c_send, c_recv, zb, levels), (l_send, l_recv, 0, zb))
+        for phase, (source, target, low, stop) in enumerate(parts):
+            projected = product(vector[...], basis[:, 128 * low:128 * stop], NN)
+            for j in range(nz):
+                for at in range(stop - low):
+                    source[t, j, own * at:own * at + own, :] = (
+                        projected[own * j:own * j + own, 128 * at:128 * at + 128])
+            if t == 0 and phase == 0:
+                pl.semaphore_wait(barrier, len(partners))
+            for step in z_steps:
+                peer = lax.rem(z + step, nz)
+                send(source.at[t, peer], target.at[t, z], t, phase, z_device(step))
         c_recv[t, z] = c_send[t, z]
         l_recv[t, z] = l_send[t, z]
 
@@ -211,7 +210,7 @@
         rr = jnp.zeros((rhs_count, 1), F32)
         rn = jnp.zeros((rhs_count, 1), F32)
         cross = jnp.zeros((rhs_count, 1), F32)
-        for low, width in spans(leaf, 384):
+        for low, width in spans(leaf, 512):
             columns = pl.ds(low, width)
             near_now = product(halves[...], blocks[:, columns], NN)
             near[:, columns] = near_now
@@ -253,10 +252,26 @@
         node_sums, _, products = tree_steps(found, 0, own)
         return node_sums, products
 
+    def transpose_bases(first, stop):
+        for level in range(first, stop):
+            for low, width in spans(leaf, 128):
+                part = basis[pl.ds(low, width), 128 * level:128 * level + 128].astype(F32)
+                basis_t[128 * level:128 * level + 128, pl.ds(low, width)] = part.T.astype(BF16)
+
+    def gather_siblings(source, t, first, stop):
+        for j in range(nz):
+            for level in range(first, stop):
+                at = own * (level - first)
+                sib_f32[own * j:own * j + own, 128 * level:128 * level + 128] = (
+                    source[t, j, at:at + own, :])
+        columns = slice(128 * first, 128 * stop)
+        high, small = split(sib_f32[:, columns])
+        sib_halves[:, columns] = jnp.concatenate([high, small], axis=0)
+
     def siblings(t, owned):
         if t == 0:
             loads[levels + 2].wait()
-        packed = near_and_dots(t == 0)
+        packed = near_and_dots(True) if t == 0 else None
         total = upper_sums(t, owned)
         for bit in range(yb + hb):
             x_send[t, bit] = total[own * bit:own * bit + own]
@@ -264,7 +279,6 @@
             bit = mask.bit_length() - 1
             send(x_send.at[t, bit], x_recv.at[t, mask], t, 9, x_device(mask))
         node_sums, products = lower_sums(t, owned)
-        packed = add_dots(packed, products)
         for j in range(nz):
             for level in range(zb):
                 rows = slice(own * level, own * level + own)
@@ -273,7 +287,11 @@
             peer = lax.rem(z + step, nz)
             send(a_send.at[t, peer], a_recv.at[t, z], t, 4, z_device(step))
         a_recv[t, z] = a_send[t, z]
-
+        if t == 0:
+            transpose_bases(0, levels // 2)
+        else:
+            packed = near_and_dots(False)
+        packed = add_dots(packed, products)
         await_recv(x_recv.at[t, pl.ds(1, nh * ny - 1)], t, 9)
         for bit in range(yb + hb):
             b_send[t, own * bit:own * bit + own] = sum(
@@ -285,6 +303,13 @@
         s_send[t, 0] = packed
         for mask in masks:
             send(s_send.at[t, 0], sx_recv.at[t, mask], t, 10, x_device(mask))
+        if t == 0:
+            transpose_bases(levels // 2, levels)
+        await_recv(a_recv.at[t, pl.ds(0, nz - 1)], t, 4)
+        gather_siblings(a_recv, t, 0, zb)
+        for low, width in spans(leaf, 512):
+            columns = pl.ds(low, width)
+            far[:, columns] = product(sib_halves[:, :128 * zb], basis_t[:128 * zb, columns], NN)
         if t > 0:
             for number in range(3):
                 place_chunk(number)
@@ -296,18 +321,12 @@
             send(s_send.at[t, 1], sz_recv.at[t, z], t, 8, z_device(step))
         sz_recv[t, z] = packed
 
-        await_recv(a_recv.at[t, pl.ds(0, nz - 1)], t, 4)
         await_recv(b_recv.at[t, pl.ds(0, nz - 1)], t, 7)
-        for j in range(nz):
-            for level in range(levels):
-                source, at = (a_recv, level) if level < zb else (b_recv, level - zb)
-                sib_f32[own * j:own * j + own, 128 * level:128 * level + 128] = (
-                    source[t, j, own * at:own * at + own, :])
-        high, small = split(sib_f32[...])
-        sib_halves[...] = jnp.concatenate([high, small], axis=0)
-        for low, width in spans(leaf, 384):
+        gather_siblings(b_recv, t, zb, levels)
+        for low, width in spans(leaf, 512):
             columns = pl.ds(low, width)
-            far_now = product(sib_halves[...], basis[columns, :], NT)
+            upper_part = product(sib_halves[:, 128 * zb:], basis_t[128 * zb:, columns], NN)
+            far_now = far[:, columns] + upper_part
             far[:, columns] = far_now
             high, small = split(near[:, columns] + far_now)
             sent[:, columns] = jnp.concatenate([high, small], axis=0)
@@ -438,6 +457,7 @@
         pltpu.VMEM((1, leaf), jnp.int32),
         pltpu.VMEM((leaf, leaf), BF16),
         pltpu.VMEM((leaf, 128 * levels), BF16),
+        pltpu.VMEM((128 * levels, leaf), BF16),
         pltpu.VMEM((leaf, leaf), BF16),
         pltpu.VMEM((2 * rhs_count, leaf), BF16),
         pltpu.VMEM((rhs_count, 128 * levels), F32),

time: 64.5 us -> 62.1 us (0.963)
  Pallas kernels: 62.8 us -> 60.3 us
    pallas_call x1, Pallas kernels: 62.8 us -> 60.3 us  [per_device(): pl.pallas_call(functools.partial(kernel, dims), out_shape=jax.ShapeDtypeS...]
where the time goes in v4:
time: 62.1 us; the launch traced here: 62 us
  Pallas kernels  60.3 us (97%)
  local copies, waits for them, and re-layouts  1.65 us (3%)
    pallas_call x1, Pallas kernels, per_device(): pl.pallas_call(functools.partial(kernel, dims), out_shape=jax.ShapeDtypeS...  60.3 us
    unnamed x1, local copies, waits for them, and re-layouts  1.65 us

profile of v4, /device:TPU:1, one launch (start us, length us, event | category | flops | bytes accessed | tf_op | source)
XLA Modules:
  0.0 62.0 jit_solution(3270892052609244865)
XLA Ops:
  0.0 60.3 %tree_cg.1 = f32[32,1920]{1,0:T(8,128)} custom-call(bf16[32,1920]{1,0:T(8,128)(2,1)} %rhs_hbm.1, s32[1,1920]{1,0:T(1,128)} %order_hbm.1, bf16[1920,1920]{1,0:T(8,128)(2,1)} %leaf_hbm.1, bf16[8,1920,128]{2,1,0:T(8,128)(2,1)} %bases_hbm.1), custom_call_target="tpu_custom_call" | custom-call | tf_op jit(solution)/shard_map/tree_cg/pallas_call | solution.py:480
  60.3 1.7 %copy.6 = f32[32,1920]{1,0:T(8,128)} copy(f32[32,1920]{1,0:T(8,128)} %tree_cg.1) | data formatting | bytes 491520
